TPU v7x, 32 devices: a whole 2x2x4 slice. The times are simulated.
32 devices in a mesh: slab: 8 (over y, x, core), orb: 4 (over z).
Axes of the slice: x: 2, y: 2, z: 4, core: 2. Of those that a mesh axis runs over, the one named last changes fastest.
Arguments:
- inverses: bfloat16 [8, 4, 2, 8, 512, 512], P('slab', None, None, 'orb'), may hold values from -0.5 to 1.5
- coupling: bfloat16 [8, 2, 32, 3, 128, 128], P('slab', None, 'orb'), may hold values from -0.21875 to 0.21875
- pattern: int32 [8, 32, 3], P('slab', 'orb'), may hold values 0 or 1
- left_lead: bfloat16 [4, 2, 64, 4096], P(None, None, None, 'orb'), may hold values from -6 to 6
- right_lead: bfloat16 [4, 2, 64, 4096], P(None, None, None, 'orb'), may hold values from -6 to 6
- potential: float32 [8, 4096], P('slab', 'orb'), may hold values from -0.5 to 0.5
- fermi_weight: float32 [64], replicated, may hold values from 0.1 to 1
- energy_index: int32 [4], replicated, may hold values from 0 to 63
- owner_map: int32 [8, 512, 1], P('slab', 'orb'), may hold values from 0 to 7; in each aligned block of 128 rows (0 to 127, 128 to 255, ..., all dimensions but the last counted through in order) at most 16 rows name the same one
Outputs:
- green_carry: bfloat16 [8, 4, 2, 64, 4096], P('slab', None, None, None, 'orb')
- owner_rows: float32 [8, 8, 64, 8, 128], P('slab', None, 'orb')
Inputs may be any that keep to these rules, and one draw needn't show every extreme that they name: `owner_map`: among the atoms of one device (aligned runs of 128 atoms of a slab) at most 16 name the same owner, and exactly 16 do in some run.
All inputs are finite; a program needn't handle non-finite values. No bound on the sum of `pattern` on one device may be relied on, other than what follows from the above.
Results may differ from a plain program's by a relative error of at most 0.04.
Values may be sent and summed in bfloat16 or wider, within the bound.
A program may use at most 128 MiB of HBM per device.

v0:
```python
import jax
import jax.numpy as jnp
from jax import lax
from jax.sharding import PartitionSpec as P

ATOM_ORB = 8
SCAP = 16


def shifted(shard, axis, by):
    peers = lax.axis_size(axis)
    pairs = [(i, i + by) for i in range(peers) if 0 <= i + by < peers]
    return lax.ppermute(shard, axis, pairs)


def extended_2(block, sides, width):
    for axis, dim in sides:
        count = lax.axis_size(axis)
        forward = [(i, i + 1) for i in range(count - 1)]
        backward = [(target, source) for source, target in forward]
        low = lax.ppermute(
            lax.slice_in_dim(block, block.shape[dim] - width, None, axis=dim), axis, forward
        )
        high = lax.ppermute(lax.slice_in_dim(block, 0, width, axis=dim), axis, backward)
        block = jnp.concatenate([low, block, high], axis=dim)
    return block


def settle(value):
    return lax.optimization_barrier(value.astype(jnp.bfloat16))


def through_inverse(blocks, carry):
    energies, _, modes, orbitals = carry.shape
    block_count = blocks.shape[2]
    block_size = blocks.shape[3]
    parted = carry.reshape(energies, 2, modes, block_count, block_size)

    def product(left_side, right_side):
        return jnp.einsum(
            "ecgp,egop->ecgo", left_side, right_side, preferred_element_type=jnp.float32
        )

    real_out = product(parted[:, 0], blocks[:, 0]) - product(parted[:, 1], blocks[:, 1])
    imag_out = product(parted[:, 0], blocks[:, 1]) + product(parted[:, 1], blocks[:, 0])
    return jnp.stack([real_out, imag_out], 1).reshape(energies, 2, modes, orbitals)


def born_map(blocks, potential_row, carry):
    gained = settle(through_inverse(blocks, carry))
    mixed = settle(carry.astype(jnp.float32) + potential_row * gained.astype(jnp.float32))
    return through_inverse(blocks, mixed)


def couple_extended(masked, extended, orbitals):
    energies, _, modes, _ = extended.shape
    block_width = masked.shape[-1]
    nblocks = orbitals // block_width
    windows = jnp.stack(
        [
            extended[..., offset * block_width : offset * block_width + orbitals]
            for offset in range(3)
        ],
        3,
    )
    windows = windows.reshape(energies, 2, modes, 3, nblocks, block_width)

    def product(left_side, right_side):
        return jnp.einsum(
            "ecdrp,rdop->ecro", left_side, right_side, preferred_element_type=jnp.float32
        )

    real_out = product(windows[:, 0], masked[0]) - product(windows[:, 1], masked[1])
    imag_out = product(windows[:, 0], masked[1]) + product(windows[:, 1], masked[0])
    return jnp.stack([real_out, imag_out], 1).reshape(energies, 2, modes, orbitals)


def couple_spread(masked, carry):
    energies, _, modes, orbitals = carry.shape
    block_width = masked.shape[-1]
    nblocks = orbitals // block_width
    parted = carry.reshape(energies, 2, modes, nblocks, block_width)

    def product(left_side, right_side):
        return jnp.einsum(
            "ecro,rdop->ecrdp", left_side, right_side, preferred_element_type=jnp.float32
        )

    real_out = product(parted[:, 0], masked[0]) + product(parted[:, 1], masked[1])
    imag_out = product(parted[:, 1], masked[0]) - product(parted[:, 0], masked[1])
    both = jnp.stack([real_out, imag_out], 1)
    spread = jnp.zeros((energies, 2, modes, orbitals + 2 * block_width), jnp.float32)
    for offset in range(3):
        piece = both[:, :, :, :, offset, :].reshape(energies, 2, modes, orbitals)
        spread = spread + jnp.pad(
            piece, ((0, 0), (0, 0), (0, 0), (offset * block_width, (2 - offset) * block_width))
        )
    return spread


def forward_step(blocks, masked, potential_row, extended, orbitals):
    entering = settle(couple_extended(masked, extended, orbitals))
    return born_map(blocks, potential_row, entering).astype(jnp.bfloat16)


def backward_step(blocks, masked, potential_row, forward_part, entering):
    green_now = (
        forward_part.astype(jnp.float32) + born_map(blocks, potential_row, entering)
    ).astype(jnp.bfloat16)
    return (green_now, couple_spread(masked, green_now))


def split_rims(spread, orbitals, block_width):
    middle = spread[..., block_width : block_width + orbitals]
    rims_out = jnp.concatenate(
        [spread[..., :block_width], spread[..., orbitals + block_width :]], -1
    )
    return (middle, rims_out)


def join_rims(middle, arrived, block_width):
    folded = middle.at[..., :block_width].add(arrived[..., :block_width])
    folded = folded.at[..., -block_width:].add(arrived[..., 3 * block_width :])
    return settle(folded)


def shards(
    inverses,
    coupling,
    pattern,
    left_lead,
    right_lead,
    potential,
    fermi_weight,
    energy_index,
    owner_map,
):
    masked = coupling[0] * pattern[0][None, :, :, None, None].astype(jnp.bfloat16)
    block_width = coupling.shape[-1]
    orbitals = left_lead.shape[-1]
    energies = left_lead.shape[0]
    slabs = lax.axis_size("slab")
    position = lax.axis_index("slab")
    leading = position == 0
    trailing = position == slabs - 1
    blocks = inverses[0]
    potential_row = potential[0]

    def forward_turn(step_index, stored):
        arrived = shifted(stored, "slab", 1)
        entering = jnp.where(leading, left_lead, arrived)
        extended = extended_2(entering, (("orb", 3),), block_width)
        return lax.cond(
            position == step_index,
            lambda: forward_step(blocks, masked, potential_row, extended, orbitals),
            lambda: stored,
        )

    forward_all = lax.fori_loop(0, slabs, forward_turn, jnp.zeros_like(left_lead))
    spread_shape = left_lead.shape[:-1] + (orbitals + 2 * block_width,)

    def backward_turn(step_index, carried):
        green_rows, outgoing = carried
        arrived = shifted(outgoing, "slab", -1)
        entering = jnp.where(trailing, right_lead, arrived)
        active = position == slabs - 1 - step_index
        fresh, spread = lax.cond(
            active,
            lambda: backward_step(blocks, masked, potential_row, forward_all, entering),
            lambda: (green_rows, jnp.zeros(spread_shape, jnp.float32)),
        )
        middle, rims_out = split_rims(spread, orbitals, block_width)
        arrived_rims = extended_2(rims_out, (("orb", 3),), block_width)
        folded = join_rims(middle, arrived_rims, block_width)
        return (fresh, jnp.where(active, folded, outgoing))

    green_rows, _ = lax.fori_loop(
        0, slabs, backward_turn, (jnp.zeros_like(left_lead), jnp.zeros_like(left_lead))
    )
    grid_points = jnp.arange(fermi_weight.shape[0], dtype=jnp.int32)
    weights = jnp.sum(
        jnp.where(grid_points[None, :] == energy_index[:, None], fermi_weight[None, :], 0.0), 1
    )
    nblocks = orbitals // block_width
    modes = green_rows.shape[2]
    parted = green_rows.reshape(energies, 2, modes, nblocks, block_width)
    inner_sum = jnp.einsum("eqcbo,eqcbp->ebop", parted, parted, preferred_element_type=jnp.float32)
    response = jnp.einsum("e,ebop->bop", weights, inner_sum, precision=lax.Precision.HIGHEST) / (
        2.0 * modes
    )
    payload = response.reshape(-1, ATOM_ORB, block_width)
    owners = owner_map[0, :, 0]
    targets = jnp.arange(slabs, dtype=jnp.int32)
    matches = (owners[:, None] == targets[None, :]).astype(jnp.int32)
    ranking = jnp.sum((jnp.cumsum(matches, 0) - 1) * matches, 1)
    slot_ids = jnp.arange(SCAP, dtype=jnp.int32)
    selection = (
        (owners[None, None, :] == targets[:, None, None])
        & (ranking[None, None, :] == slot_ids[None, :, None])
    ).astype(jnp.float32)
    sending = jnp.einsum("osa,axy->osxy", selection, payload, precision=lax.Precision.HIGHEST)
    received = lax.all_to_all(
        sending.astype(jnp.bfloat16), "slab", split_axis=0, concat_axis=0, tiled=True
    ).astype(sending.dtype)
    return (green_rows[None], received[None])


def solution(mesh):
    in_specs = (
        P("slab", None, None, "orb", None, None),
        P("slab", None, "orb", None, None, None),
        P("slab", "orb", None),
        P(None, None, None, "orb"),
        P(None, None, None, "orb"),
        P("slab", "orb"),
        P(),
        P(),
        P("slab", "orb", None),
    )
    out_specs = (P("slab", None, None, None, "orb"), P("slab", None, "orb", None, None))
    return jax.shard_map(shards, mesh=mesh, in_specs=in_specs, out_specs=out_specs, check_vma=False)
```

profile of v0, /device:TPU:0, one launch (start us, length us, event | category | flops | bytes accessed | tf_op | source)
XLA Modules:
  0.0 1485.7 jit_solution(4483608750079569970)
XLA Ops:
  3.2 7.6 copy.189
  15.8 395.2 %while.39 = (s32[]{:T(128)}, bf16[4,2,64,1024]{3,2,0,1:T(8,128)(2,1)}, s32[]{:T(128)}, pred[]{:T(512)}, bf16[4,2,64,1024]{3,2,0,1:T(8,128)(2,1)}, /*index=5*/bf1...) while((s32[]{:T(128)}, ...), condition=%wide.region_3.4_spmd, body=%wide.region_0.3_spmd.sunk | while | flops 2964586496 | bytes 155193776 | solution.py:159
  24.4 4.9 collective-permute-start.2
  32.0 59.1 %conditional.5 = (bf16[4,2,64,1024]{3,2,0,1:T(8,128)(2,1)}) conditional(s32[]{:T(128)} %convert_element_type.99, bf16[4,2,64,1024]{3,2,0,1:T(8,128)(2,1)} %get-tuple-element.767, (bf16[4,2,64,1280]{3,2,1,0:T(8,128)(2,1)S(1)}, bf16[4,2,64,1024]{3,2,1,0:T(8,128)(2,1)S(1)}, bf16[2,8,3,128,128]{4,3,2,1,0:T(8,128)(2,1)S(1)}, f32[1,1024]{1,0:T(1,128)S(1)}, ...), branch_computations={%region_1.1_spmd, %region_2.2_spmd} | conditional | flops 2960130048 | bytes 141562016 | solution.py:153
  98.7 5.0 collective-permute-start.2
  108.5 60.6 %collective-permute-start = (bf16[4,2,64,1024]{3,2,1,0:T(8,128)(2,1)S(1)}, bf16[4,2,64,1024]{3,2,1,0:T(8,128)(2,1)S(1)}, u32[]{:S(2)}, u32[]{:S(2)}) collective-permute-start(bf16[4,2,64,1024]{3,2,1,0:T(8,128)(2,1)S(1)} %copy.194), channel_id=1, source_target_pairs={{0,4},{4,8},{8,12},{12,16},{16,20},{20,24},{24,28},{1,5},{5,9},{9,... | collective-permute-start | bytes 3145736 | tf_op jit(solution)/shard_map/while/body/eval_jaxpr/ppermute | solution.py:13
  174.0 5.0 collective-permute-start.2
  183.0 10.6 collective-permute-start
  198.5 4.7 collective-permute-start.2
  207.3 73.2 %collective-permute-start = (bf16[4,2,64,1024]{3,2,1,0:T(8,128)(2,1)S(1)}, bf16[4,2,64,1024]{3,2,1,0:T(8,128)(2,1)S(1)}, u32[]{:S(2)}, u32[]{:S(2)}) collective-permute-start(bf16[4,2,64,1024]{3,2,1,0:T(8,128)(2,1)S(1)} %copy.194), channel_id=1, source_target_pairs={{0,4},{4,8},{8,12},{12,16},{16,20},{20,24},{24,28},{1,5},{5,9},{9,... | collective-permute-start | bytes 3145736 | tf_op jit(solution)/shard_map/while/body/eval_jaxpr/ppermute | solution.py:13
  285.4 4.7 collective-permute-start.2
  294.1 14.2 collective-permute-start
  313.2 4.7 collective-permute-start.2
  322.0 48.9 %collective-permute-start = (bf16[4,2,64,1024]{3,2,1,0:T(8,128)(2,1)S(1)}, bf16[4,2,64,1024]{3,2,1,0:T(8,128)(2,1)S(1)}, u32[]{:S(2)}, u32[]{:S(2)}) collective-permute-start(bf16[4,2,64,1024]{3,2,1,0:T(8,128)(2,1)S(1)} %copy.194), channel_id=1, source_target_pairs={{0,4},{4,8},{8,12},{12,16},{16,20},{20,24},{24,28},{1,5},{5,9},{9,... | collective-permute-start | bytes 3145736 | tf_op jit(solution)/shard_map/while/body/eval_jaxpr/ppermute | solution.py:13
  375.8 4.7 collective-permute-start.2
  384.5 14.2 collective-permute-start
  403.6 4.7 collective-permute-start.2
  412.1 1053.8 %while.40 = (s32[]{:T(128)}, bf16[4,2,64,1024]{3,2,0,1:T(8,128)(2,1)}, bf16[4,2,64,1024]{3,2,1,0:T(8,128)(2,1)}, s32[]{:T(128)}, bf16[4,2,64,1024]{3,2,0,1:T(8,1...) while((s32[]{:T(128)}, ...), condition=%wide.region_7.8_spmd.clone, body=%wide.region_4.7_spmd.clone.sunk | while | flops 2966814720 | bytes 208671280 | solution.py:177
  429.2 71.4 %collective-permute-done.3 = bf16[4,2,64,1024]{3,2,1,0:T(8,128)(2,1)} collective-permute-done((bf16[4,2,64,1024]{3,2,1,0:T(8,128)(2,1)S(1)}, bf16[4,2,64,1024]{3,2,1,0:T(8,128)(2,1)}, u32[]{:S(2)}, u32[]{:S(2)}) %collective-permute-start.3) | collective-permute-done | bytes 1048608 | tf_op jit(solution)/shard_map/while/body/eval_jaxpr/ppermute | solution.py:13
  501.6 4.1 collective-permute-start.4
  509.9 4.1 collective-permute-done.5
  518.8 23.1 %collective-permute-done.3 = bf16[4,2,64,1024]{3,2,1,0:T(8,128)(2,1)} collective-permute-done((bf16[4,2,64,1024]{3,2,1,0:T(8,128)(2,1)S(1)}, bf16[4,2,64,1024]{3,2,1,0:T(8,128)(2,1)}, u32[]{:S(2)}, u32[]{:S(2)}) %collective-permute-start.3) | collective-permute-done | bytes 1048608 | tf_op jit(solution)/shard_map/while/body/eval_jaxpr/ppermute | solution.py:13
  551.0 4.1 collective-permute-done.5
  560.0 48.1 %collective-permute-done.3 = bf16[4,2,64,1024]{3,2,1,0:T(8,128)(2,1)} collective-permute-done((bf16[4,2,64,1024]{3,2,1,0:T(8,128)(2,1)S(1)}, bf16[4,2,64,1024]{3,2,1,0:T(8,128)(2,1)}, u32[]{:S(2)}, u32[]{:S(2)}) %collective-permute-start.3) | collective-permute-done | bytes 1048608 | tf_op jit(solution)/shard_map/while/body/eval_jaxpr/ppermute | solution.py:13
  625.8 16.6 %collective-permute-done.3 = bf16[4,2,64,1024]{3,2,1,0:T(8,128)(2,1)} collective-permute-done((bf16[4,2,64,1024]{3,2,1,0:T(8,128)(2,1)S(1)}, bf16[4,2,64,1024]{3,2,1,0:T(8,128)(2,1)}, u32[]{:S(2)}, u32[]{:S(2)}) %collective-permute-start.3) | collective-permute-done | bytes 1048608 | tf_op jit(solution)/shard_map/while/body/eval_jaxpr/ppermute | solution.py:13
  658.7 62.8 %collective-permute-done.3 = bf16[4,2,64,1024]{3,2,1,0:T(8,128)(2,1)} collective-permute-done((bf16[4,2,64,1024]{3,2,1,0:T(8,128)(2,1)S(1)}, bf16[4,2,64,1024]{3,2,1,0:T(8,128)(2,1)}, u32[]{:S(2)}, u32[]{:S(2)}) %collective-permute-start.3) | collective-permute-done | bytes 1048608 | tf_op jit(solution)/shard_map/while/body/eval_jaxpr/ppermute | solution.py:13
  737.8 15.4 %collective-permute-done.3 = bf16[4,2,64,1024]{3,2,1,0:T(8,128)(2,1)} collective-permute-done((bf16[4,2,64,1024]{3,2,1,0:T(8,128)(2,1)S(1)}, bf16[4,2,64,1024]{3,2,1,0:T(8,128)(2,1)}, u32[]{:S(2)}, u32[]{:S(2)}) %collective-permute-start.3) | collective-permute-done | bytes 1048608 | tf_op jit(solution)/shard_map/while/body/eval_jaxpr/ppermute | solution.py:13
  769.5 48.6 %collective-permute-done.3 = bf16[4,2,64,1024]{3,2,1,0:T(8,128)(2,1)} collective-permute-done((bf16[4,2,64,1024]{3,2,1,0:T(8,128)(2,1)S(1)}, bf16[4,2,64,1024]{3,2,1,0:T(8,128)(2,1)}, u32[]{:S(2)}, u32[]{:S(2)}) %collective-permute-start.3) | collective-permute-done | bytes 1048608 | tf_op jit(solution)/shard_map/while/body/eval_jaxpr/ppermute | solution.py:13
  834.5 540.9 %collective-permute-done.3 = bf16[4,2,64,1024]{3,2,1,0:T(8,128)(2,1)} collective-permute-done((bf16[4,2,64,1024]{3,2,1,0:T(8,128)(2,1)S(1)}, bf16[4,2,64,1024]{3,2,1,0:T(8,128)(2,1)}, u32[]{:S(2)}, u32[]{:S(2)}) %collective-permute-start.3) | collective-permute-done | bytes 1048608 | tf_op jit(solution)/shard_map/while/body/eval_jaxpr/ppermute | solution.py:13
  1375.4 77.4 %conditional.6 = (bf16[4,2,64,1024]{3,2,0,1:T(8,128)(2,1)}, f32[4,2,64,1280]{3,2,1,0:T(8,128)S(1)}) conditional(s32[]{:T(128)} %convert_element_type.100, bf16[4,2,64,1024]{3,2,0,1:T(8,128)(2,1)} %get-tuple-element.798, (bf16[4,2,64,1024]{3,2,0,1:T(8,128)(2,1)}, pred[]{:T(512)}, bf16[4,2,64,1024]{3,2,0,1:T(8,128)(2,1)}, ...), branch_computations={%region_5.5_spmd, %region_6.6_spmd} | conditional | flops 2964586496 | bytes 166203504 | solution.py:167
  1468.1 4.3 fusion.150
  1478.5 5.8 all-to-all-done
  (379 shorter events, 351.4 us)
Async XLA Ops:
  23.1 7.3 collective-permute-start.1
  24.4 7.5 collective-permute-start.2
  97.4 8.4 collective-permute-start.1
  98.7 8.3 collective-permute-start.2
  108.5 62.8 %collective-permute-start = (bf16[4,2,64,1024]{3,2,1,0:T(8,128)(2,1)S(1)}, bf16[4,2,64,1024]{3,2,1,0:T(8,128)(2,1)S(1)}, u32[]{:S(2)}, u32[]{:S(2)}) collective-permute-start(bf16[4,2,64,1024]{3,2,1,0:T(8,128)(2,1)S(1)} %copy.194), channel_id=1, source_target_pairs={{0,4},{4,8},{8,12},{12,16},{16,20},{20,24},{24,28},{1,5},{5,9},{9,... | collective-permute-start | bytes 3145736 | tf_op jit(solution)/shard_map/while/body/eval_jaxpr/ppermute | solution.py:13
  172.7 7.3 collective-permute-start.1
  174.0 7.5 collective-permute-start.2
  183.0 12.8 collective-permute-start
  207.3 75.4 %collective-permute-start = (bf16[4,2,64,1024]{3,2,1,0:T(8,128)(2,1)S(1)}, bf16[4,2,64,1024]{3,2,1,0:T(8,128)(2,1)S(1)}, u32[]{:S(2)}, u32[]{:S(2)}) collective-permute-start(bf16[4,2,64,1024]{3,2,1,0:T(8,128)(2,1)S(1)} %copy.194), channel_id=1, source_target_pairs={{0,4},{4,8},{8,12},{12,16},{16,20},{20,24},{24,28},{1,5},{5,9},{9,... | collective-permute-start | bytes 3145736 | tf_op jit(solution)/shard_map/while/body/eval_jaxpr/ppermute | solution.py:13
  294.1 16.4 %collective-permute-start = (bf16[4,2,64,1024]{3,2,1,0:T(8,128)(2,1)S(1)}, bf16[4,2,64,1024]{3,2,1,0:T(8,128)(2,1)S(1)}, u32[]{:S(2)}, u32[]{:S(2)}) collective-permute-start(bf16[4,2,64,1024]{3,2,1,0:T(8,128)(2,1)S(1)} %copy.194), channel_id=1, source_target_pairs={{0,4},{4,8},{8,12},{12,16},{16,20},{20,24},{24,28},{1,5},{5,9},{9,... | collective-permute-start | bytes 3145736 | tf_op jit(solution)/shard_map/while/body/eval_jaxpr/ppermute | solution.py:13
  322.0 51.1 %collective-permute-start = (bf16[4,2,64,1024]{3,2,1,0:T(8,128)(2,1)S(1)}, bf16[4,2,64,1024]{3,2,1,0:T(8,128)(2,1)S(1)}, u32[]{:S(2)}, u32[]{:S(2)}) collective-permute-start(bf16[4,2,64,1024]{3,2,1,0:T(8,128)(2,1)S(1)} %copy.194), channel_id=1, source_target_pairs={{0,4},{4,8},{8,12},{12,16},{16,20},{20,24},{24,28},{1,5},{5,9},{9,... | collective-permute-start | bytes 3145736 | tf_op jit(solution)/shard_map/while/body/eval_jaxpr/ppermute | solution.py:13
  384.5 16.4 %collective-permute-start = (bf16[4,2,64,1024]{3,2,1,0:T(8,128)(2,1)S(1)}, bf16[4,2,64,1024]{3,2,1,0:T(8,128)(2,1)S(1)}, u32[]{:S(2)}, u32[]{:S(2)}) collective-permute-start(bf16[4,2,64,1024]{3,2,1,0:T(8,128)(2,1)S(1)} %copy.194), channel_id=1, source_target_pairs={{0,4},{4,8},{8,12},{12,16},{16,20},{20,24},{24,28},{1,5},{5,9},{9,... | collective-permute-start | bytes 3145736 | tf_op jit(solution)/shard_map/while/body/eval_jaxpr/ppermute | solution.py:13
  427.9 72.7 %collective-permute-start.3 = (bf16[4,2,64,1024]{3,2,1,0:T(8,128)(2,1)S(1)}, bf16[4,2,64,1024]{3,2,1,0:T(8,128)(2,1)}, u32[]{:S(2)}, u32[]{:S(2)}) collective-permute-start(bf16[4,2,64,1024]{3,2,1,0:T(8,128)(2,1)S(1)} %broadcast_select_fusion.4), channel_id=1, source_target_pairs={{4,0},{8,4},{12,8},{16,12},{20,16},{24,20},{28,24},{5,1},{9,5},{13... | collective-permute-start | bytes 3145736 | tf_op jit(solution)/shard_map/while/body/eval_jaxpr/ppermute | solution.py:13
  501.6 8.2 collective-permute-start.4
  505.7 8.3 collective-permute-start.5
  517.5 24.4 %collective-permute-start.3 = (bf16[4,2,64,1024]{3,2,1,0:T(8,128)(2,1)S(1)}, bf16[4,2,64,1024]{3,2,1,0:T(8,128)(2,1)}, u32[]{:S(2)}, u32[]{:S(2)}) collective-permute-start(bf16[4,2,64,1024]{3,2,1,0:T(8,128)(2,1)S(1)} %broadcast_select_fusion.4), channel_id=1, source_target_pairs={{4,0},{8,4},{12,8},{16,12},{20,16},{24,20},{28,24},{5,1},{9,5},{13... | collective-permute-start | bytes 3145736 | tf_op jit(solution)/shard_map/while/body/eval_jaxpr/ppermute | solution.py:13
  542.9 8.1 collective-permute-start.4
  546.8 8.3 collective-permute-start.5
  558.7 49.4 %collective-permute-start.3 = (bf16[4,2,64,1024]{3,2,1,0:T(8,128)(2,1)S(1)}, bf16[4,2,64,1024]{3,2,1,0:T(8,128)(2,1)}, u32[]{:S(2)}, u32[]{:S(2)}) collective-permute-start(bf16[4,2,64,1024]{3,2,1,0:T(8,128)(2,1)S(1)} %broadcast_select_fusion.4), channel_id=1, source_target_pairs={{4,0},{8,4},{12,8},{16,12},{20,16},{24,20},{28,24},{5,1},{9,5},{13... | collective-permute-start | bytes 3145736 | tf_op jit(solution)/shard_map/while/body/eval_jaxpr/ppermute | solution.py:13
  609.1 7.8 collective-permute-start.4
  612.7 8.3 collective-permute-start.5
  624.5 17.9 %collective-permute-start.3 = (bf16[4,2,64,1024]{3,2,1,0:T(8,128)(2,1)S(1)}, bf16[4,2,64,1024]{3,2,1,0:T(8,128)(2,1)}, u32[]{:S(2)}, u32[]{:S(2)}) collective-permute-start(bf16[4,2,64,1024]{3,2,1,0:T(8,128)(2,1)S(1)} %broadcast_select_fusion.4), channel_id=1, source_target_pairs={{4,0},{8,4},{12,8},{16,12},{20,16},{24,20},{28,24},{5,1},{9,5},{13... | collective-permute-start | bytes 3145736 | tf_op jit(solution)/shard_map/while/body/eval_jaxpr/ppermute | solution.py:13
  645.6 8.3 collective-permute-start.5
  657.4 64.1 %collective-permute-start.3 = (bf16[4,2,64,1024]{3,2,1,0:T(8,128)(2,1)S(1)}, bf16[4,2,64,1024]{3,2,1,0:T(8,128)(2,1)}, u32[]{:S(2)}, u32[]{:S(2)}) collective-permute-start(bf16[4,2,64,1024]{3,2,1,0:T(8,128)(2,1)S(1)} %broadcast_select_fusion.4), channel_id=1, source_target_pairs={{4,0},{8,4},{12,8},{16,12},{20,16},{24,20},{28,24},{5,1},{9,5},{13... | collective-permute-start | bytes 3145736 | tf_op jit(solution)/shard_map/while/body/eval_jaxpr/ppermute | solution.py:13
  724.7 8.3 collective-permute-start.5
  736.5 16.7 %collective-permute-start.3 = (bf16[4,2,64,1024]{3,2,1,0:T(8,128)(2,1)S(1)}, bf16[4,2,64,1024]{3,2,1,0:T(8,128)(2,1)}, u32[]{:S(2)}, u32[]{:S(2)}) collective-permute-start(bf16[4,2,64,1024]{3,2,1,0:T(8,128)(2,1)S(1)} %broadcast_select_fusion.4), channel_id=1, source_target_pairs={{4,0},{8,4},{12,8},{16,12},{20,16},{24,20},{28,24},{5,1},{9,5},{13... | collective-permute-start | bytes 3145736 | tf_op jit(solution)/shard_map/while/body/eval_jaxpr/ppermute | solution.py:13
  756.4 8.3 collective-permute-start.5
  768.2 49.9 %collective-permute-start.3 = (bf16[4,2,64,1024]{3,2,1,0:T(8,128)(2,1)S(1)}, bf16[4,2,64,1024]{3,2,1,0:T(8,128)(2,1)}, u32[]{:S(2)}, u32[]{:S(2)}) collective-permute-start(bf16[4,2,64,1024]{3,2,1,0:T(8,128)(2,1)S(1)} %broadcast_select_fusion.4), channel_id=1, source_target_pairs={{4,0},{8,4},{12,8},{16,12},{20,16},{24,20},{28,24},{5,1},{9,5},{13... | collective-permute-start | bytes 3145736 | tf_op jit(solution)/shard_map/while/body/eval_jaxpr/ppermute | solution.py:13
  821.3 8.3 collective-permute-start.5
  833.1 542.2 %collective-permute-start.3 = (bf16[4,2,64,1024]{3,2,1,0:T(8,128)(2,1)S(1)}, bf16[4,2,64,1024]{3,2,1,0:T(8,128)(2,1)}, u32[]{:S(2)}, u32[]{:S(2)}) collective-permute-start(bf16[4,2,64,1024]{3,2,1,0:T(8,128)(2,1)S(1)} %broadcast_select_fusion.4), channel_id=1, source_target_pairs={{4,0},{8,4},{12,8},{16,12},{20,16},{24,20},{28,24},{5,1},{9,5},{13... | collective-permute-start | bytes 3145736 | tf_op jit(solution)/shard_map/while/body/eval_jaxpr/ppermute | solution.py:13
  1455.7 8.3 collective-permute-start.5
  1474.0 10.3 all-to-all-start
  (67 other events, 1113.4 us)
where the time goes:
time: 1500 us; the launch traced here: 1490 us
  waiting for transfers between devices  924 us (62%)
  starting transfers between devices  321 us (21%)
  local copies, waits for them, and re-layouts  100 us (7%)
  matrix products  69.3 us (5%)
  other arithmetic  52.2 us (3%)
  loops' own time  18.1 us (1%)
    ppermute x16, waiting for transfers between devices, shifted(): return lax.ppermute(shard, axis, pairs)  844 us
    ppermute x16, starting transfers between devices, shifted(): return lax.ppermute(shard, axis, pairs)  236 us
    ppermute x16, starting transfers between devices, extended_2(): lax.ppermute(lax.slice_in_dim(block, block.shape[dim] - width, None, axis...  61 us
    dot_general x16, matrix products, product(): jnp.einsum('ecgp,egop->ecgo', left_side, right_side, preferred_element_ty...  57.3 us
    ppermute x16, waiting for transfers between devices, extended_2(): lax.ppermute(lax.slice_in_dim(block, 0, width, axis=dim), axis, backward)  41.5 us
    ppermute x16, waiting for transfers between devices, extended_2(): lax.ppermute(lax.slice_in_dim(block, block.shape[dim] - width, None, axis...  32 us
  transfers between devices with their start and end apart: 49, of which 49 were waited for; matrix products, arithmetic and copies ran while one was open for 0% of the time, Pallas kernels for 0%

commit v1 on v0

v1 whole, which is shorter than its diff:
```python
import functools

import jax
import jax.numpy as jnp
from jax import lax
from jax.experimental import pallas as pl
from jax.experimental.pallas import tpu as pltpu
from jax.sharding import PartitionSpec as P

ATOM_ORB = 8
SCAP = 16
F32 = jnp.float32
BF16 = jnp.bfloat16


def turned(u, conj):
    half = u.shape[0] // 2
    r, i = u[:half], u[half:]
    return jnp.concatenate([i, -r] if conj else [-i, r], 0)


def coupled(window, weight, conj):
    both = jnp.dot(window, weight, preferred_element_type=F32)
    half, width = both.shape[0] // 2, both.shape[1] // 2
    rr, ri = both[:half, :width], both[:half, width:]
    ir, ii = both[half:, :width], both[half:, width:]
    if conj:
        out = [rr + ii, ir - ri]
    else:
        out = [rr - ii, ri + ir]
    return jnp.concatenate(out, 0).astype(BF16)


def kernel(
    dims,
    inv, mf, mb, left, right, pot, fermi, eidx, own_row, own_col,
    gout, rows_out,
    ginv, xf, gf, xs, bb, stage, resp, sel, picked, sb, rb,
    inv_sem, fs, fr, bs, br, cs, cr, ls, ts, tr,
):
    S, Q, E, W, NB, BW, NG, GB = dims
    s = lax.axis_index("slab")
    q = lax.axis_index("orb")
    rows = xf.shape[1]
    first, last = s == 0, s == S - 1
    low, high = q == 0, q == Q - 1

    def to(src, dst, ssem, rsem, ds, dq):
        return pltpu.make_async_remote_copy(
            src_ref=src, dst_ref=dst, send_sem=ssem, recv_sem=rsem,
            device_id={"slab": s + ds, "orb": q + dq},
            device_id_type=pl.DeviceIdType.MESH,
        )

    def here(src, dst, sem):
        return pltpu.make_async_copy(src, dst, sem)

    def inv_copy(e):
        return here(inv.at[e], ginv.at[e], inv_sem.at[e])

    def main(buf, e, g):
        return buf.at[e, :, pl.ds(BW + g * GB, GB)]

    def halo(buf, e, side):
        return buf.at[e, :, pl.ds(0 if side == 0 else BW + W, BW)]

    def edge(src, e, side):
        return src.at[e, :, pl.ds(0 if side == 0 else W - BW, BW)]

    def coupling_copies():
        out = [(None, to(mb.at[:, 1], bb.at[:, 1], cs.at[0], cr.at[0], -1, 0))]
        n = NB - 1
        out.append((None, to(mb.at[pl.ds(1, n), 0], bb.at[pl.ds(0, n), 2], cs.at[1], cr.at[1], -1, 0)))
        out.append((None, to(mb.at[pl.ds(0, n), 2], bb.at[pl.ds(1, n), 0], cs.at[2], cr.at[2], -1, 0)))
        out.append((~low, to(mb.at[0, 0], bb.at[NB - 1, 2], cs.at[3], cr.at[3], -1, -1)))
        out.append((~high, to(mb.at[NB - 1, 2], bb.at[0, 0], cs.at[4], cr.at[4], -1, 1)))
        return out

    def wave_copies(src, dst, e, ssem, rsem, ds):
        out = []
        for g in range(NG):
            out.append((None, g, to(src.at[e, :, pl.ds(g * GB, GB)], main(dst, e, g), ssem.at[e, g], rsem.at[e, g], ds, 0)))
        out.append((~low, 0, to(edge(src, e, 0), halo(dst, e, 1), ssem.at[e, NG], rsem.at[e, NG + 1], ds, -1)))
        out.append((~high, NG - 1, to(edge(src, e, 1), halo(dst, e, 0), ssem.at[e, NG + 1], rsem.at[e, NG], ds, 1)))
        return out

    def lead_copies(e):
        return [
            (~low, to(edge(left, e, 0), halo(xf, e, 1), ls.at[e, 0], fr.at[e, NG + 1], 0, -1)),
            (~high, to(edge(left, e, 1), halo(xf, e, 0), ls.at[e, 1], fr.at[e, NG], 0, 1)),
        ]

    def guarded(cond, act):
        if cond is None:
            act()
        else:
            pl.when(cond)(act)

    def await_wave(buf, e, rsem, halos):
        for g in range(NG):
            here(main(buf, e, g), main(buf, e, g), rsem.at[e, g]).wait()
        if halos:
            for side, edge_here in ((0, low), (1, high)):
                h = halo(buf, e, side)
                pl.when(~edge_here)(lambda h=h, side=side: here(h, h, rsem.at[e, NG + side]).wait())

    def each_energy(body):
        def step(e, carry):
            body(e)
            return carry

        lax.fori_loop(0, E, step, 0)

    @each_energy
    def _(e):
        inv_copy(e).start()

    @pl.when(first)
    def _():
        @each_energy
        def _(e):
            for g in range(NG):
                here(left.at[e, :, pl.ds(g * GB, GB)], main(xf, e, g), fr.at[e, g]).start()
            for cond, copy in lead_copies(e):
                guarded(cond, copy.start)

    @pl.when(last)
    def _():
        @each_energy
        def _(e):
            for g in range(NG):
                here(right.at[e, :, pl.ds(g * GB, GB)], main(gf, e, g), br.at[e, g]).start()

    @pl.when(~first)
    def _():
        for cond, copy in coupling_copies():
            guarded(cond, copy.start)

    zero = jnp.zeros((E, rows, BW), BF16)
    zero_block = jnp.zeros((BW, 2 * BW), BF16)

    @pl.when(low)
    def _():
        xf[:, :, pl.ds(0, BW)] = zero
        gf[:, :, pl.ds(0, BW)] = zero
        bb[0, 0] = zero_block

    @pl.when(high)
    def _():
        xf[:, :, pl.ds(BW + W, BW)] = zero
        gf[:, :, pl.ds(BW + W, BW)] = zero
        bb[NB - 1, 2] = zero_block

    resp[...] = jnp.zeros(resp.shape, F32)

    atoms = own_row.shape[1]
    earlier = lax.broadcasted_iota(jnp.int32, (atoms, atoms), 0) < lax.broadcasted_iota(jnp.int32, (atoms, atoms), 1)
    same = own_col[...] == own_row[...]
    rank = jnp.sum((same & earlier).astype(F32), 0, keepdims=True)
    place = lax.broadcasted_iota(jnp.int32, (S * SCAP, atoms), 0)
    rank_i = rank.astype(jnp.int32)
    wanted = own_row[...] * SCAP + rank_i
    sel[...] = jnp.where(place == wanted, 1.0, 0.0).astype(BF16)

    def through(e, g, u):
        dn = (((1,), (1,)), ((), ()))
        return lax.dot_general(u, ginv[e, 0, g], dn, preferred_element_type=F32) + lax.dot_general(
            turned(u, False), ginv[e, 1, g], dn, preferred_element_type=F32
        )

    def born(e, g):
        u = stage[:, pl.ds(g * GB, GB)]
        gain = through(e, g, u).astype(BF16).astype(F32)
        mix = (u.astype(F32) + pot[:, pl.ds(g * GB, GB)] * gain).astype(BF16)
        return through(e, g, mix)

    def couple(buf, e, weights, conj):
        for b in range(NB):
            window = buf[e, :, pl.ds(b * BW, 3 * BW)]
            stage[:, pl.ds(b * BW, BW)] = coupled(window, weights[b].reshape(3 * BW, 2 * BW), conj)

    def forward(e):
        inv_copy(e).wait()
        await_wave(xf, e, fr, True)
        couple(xf, e, mf, False)
        copies = wave_copies(xs, xf, e, fs, fr, 1)
        for g in range(NG):
            xs[e, :, pl.ds(g * GB, GB)] = born(e, g).astype(BF16)

            @pl.when(~last)
            def _():
                for cond, after, copy in copies:
                    if after == g:
                        guarded(cond, copy.start)

    each_energy(forward)

    @pl.when(~last)
    def _():
        for i, region in enumerate((bb.at[:, 1], bb.at[pl.ds(0, NB - 1), 2], bb.at[pl.ds(1, NB - 1), 0])):
            here(region, region, cr.at[i]).wait()
        pl.when(~high)(lambda: here(bb.at[NB - 1, 2], bb.at[NB - 1, 2], cr.at[3]).wait())
        pl.when(~low)(lambda: here(bb.at[0, 0], bb.at[0, 0], cr.at[4]).wait())

    def backward(e):
        @pl.when(last)
        def _():
            await_wave(gf, e, br, False)
            stage[...] = gf[e, :, pl.ds(BW, W)]

        @pl.when(~last)
        def _():
            await_wave(gf, e, br, True)
            couple(gf, e, bb, True)

        copies = wave_copies(gout, gf, e, bs, br, -1)
        for g in range(NG):
            cols = pl.ds(g * GB, GB)
            gout[e, :, cols] = (xs[e, :, cols].astype(F32) + born(e, g)).astype(BF16)

            @pl.when(~first)
            def _():
                for cond, after, copy in copies:
                    if after == g:
                        guarded(cond, copy.start)

        weight = fermi[eidx[e]]
        for b in range(NB):
            a = gout[e, :, pl.ds(b * BW, BW)]
            gram = lax.dot_general(a, a, (((0,), (0,)), ((), ())), preferred_element_type=F32)
            resp[pl.ds(b * BW, BW), :] += weight * gram

    each_energy(backward)

    for x in range(ATOM_ORB):
        part = (resp[pl.ds(x, atoms, stride=ATOM_ORB), :] * (1.0 / rows)).astype(BF16)
        picked[pl.ds(x, S * SCAP, stride=ATOM_ORB), :] = jnp.dot(sel[...], part, preferred_element_type=F32)
    sb[...] = picked[...].reshape(sb.shape).astype(BF16)

    def tail(k):
        other = lax.rem(s + k, S)
        return pltpu.make_async_remote_copy(
            src_ref=sb.at[other], dst_ref=rb.at[s], send_sem=ts.at[k], recv_sem=tr.at[k],
            device_id={"slab": other, "orb": q}, device_id_type=pl.DeviceIdType.MESH,
        )

    for k in range(1, S):
        tail(k).start()
    rb[s] = sb[s]

    @pl.when(~first)
    def _():
        for cond, copy in coupling_copies():
            guarded(cond, copy.wait_send)

        @each_energy
        def _(e):
            for cond, _, copy in wave_copies(gout, gf, e, bs, br, -1):
                guarded(cond, copy.wait_send)

    @pl.when(first)
    def _():
        @each_energy
        def _(e):
            for cond, copy in lead_copies(e):
                guarded(cond, copy.wait_send)

    @pl.when(~last)
    def _():
        @each_energy
        def _(e):
            for cond, _, copy in wave_copies(xs, xf, e, fs, fr, 1):
                guarded(cond, copy.wait_send)

    for k in range(1, S):
        tail(k).wait_send()
    for k in range(1, S):
        source = lax.rem(s + S - k, S)
        here(rb.at[source], rb.at[source], tr.at[k]).wait()
    rows_out[...] = rb[...].astype(F32)


def shards(
    inverses, coupling, pattern, left_lead, right_lead, potential, fermi_weight, energy_index, owner_map
):
    S, Q = lax.axis_size("slab"), lax.axis_size("orb")
    E, _, modes, W = left_lead.shape
    NB, BW = coupling.shape[2], coupling.shape[-1]
    NG, GB = inverses.shape[3], inverses.shape[4]
    rows = 2 * modes
    atoms = owner_map.shape[1]
    masked = coupling[0] * pattern[0][None, :, :, None, None].astype(BF16)
    mb = masked.transpose(1, 2, 3, 0, 4).reshape(NB, 3, BW, 2 * BW)
    mf = masked.transpose(1, 2, 4, 0, 3).reshape(NB, 3, BW, 2 * BW)
    owners = owner_map.reshape(atoms)
    vm = pl.BlockSpec(memory_space=pltpu.VMEM)
    sm = pl.BlockSpec(memory_space=pltpu.SMEM)
    hbm = pl.BlockSpec(memory_space=pl.ANY)
    dma = pltpu.SemaphoreType.DMA
    green, received = pl.pallas_call(
        functools.partial(kernel, (S, Q, E, W, NB, BW, NG, GB)),
        out_shape=(
            jax.ShapeDtypeStruct((E, rows, W), BF16),
            jax.ShapeDtypeStruct((S, SCAP * ATOM_ORB, BW), F32),
        ),
        in_specs=[hbm, vm, vm, hbm, hbm, vm, sm, sm, vm, vm],
        out_specs=(vm, vm),
        scratch_shapes=[
            pltpu.VMEM((E, 2, NG, GB, GB), BF16),
            pltpu.VMEM((E, rows, W + 2 * BW), BF16),
            pltpu.VMEM((E, rows, W + 2 * BW), BF16),
            pltpu.VMEM((E, rows, W), BF16),
            pltpu.VMEM((NB, 3, BW, 2 * BW), BF16),
            pltpu.VMEM((rows, W), BF16),
            pltpu.VMEM((W, BW), F32),
            pltpu.VMEM((S * SCAP, atoms), BF16),
            pltpu.VMEM((S * SCAP * ATOM_ORB, BW), F32),
            pltpu.VMEM((S, SCAP * ATOM_ORB, BW), BF16),
            pltpu.VMEM((S, SCAP * ATOM_ORB, BW), BF16),
            dma((E,)),
            dma((E, NG + 2)),
            dma((E, NG + 2)),
            dma((E, NG + 2)),
            dma((E, NG + 2)),
            dma((5,)),
            dma((5,)),
            dma((E, 2)),
            dma((S,)),
            dma((S,)),
        ],
        compiler_params=pltpu.CompilerParams(has_side_effects=True, vmem_limit_bytes=48 * 2**20),
    )(
        inverses[0],
        mf,
        mb,
        left_lead.reshape(E, rows, W),
        right_lead.reshape(E, rows, W),
        potential,
        fermi_weight,
        energy_index,
        owners.reshape(1, atoms),
        owners.reshape(atoms, 1),
    )
    return (
        green.reshape(1, E, 2, modes, W),
        received.reshape(1, S, SCAP, ATOM_ORB, BW),
    )


def solution(mesh):
    in_specs = (
        P("slab", None, None, "orb", None, None),
        P("slab", None, "orb", None, None, None),
        P("slab", "orb", None),
        P(None, None, None, "orb"),
        P(None, None, None, "orb"),
        P("slab", "orb"),
        P(),
        P(),
        P("slab", "orb", None),
    )
    out_specs = (P("slab", None, None, None, "orb"), P("slab", None, "orb", None, None))
    return jax.shard_map(shards, mesh=mesh, in_specs=in_specs, out_specs=out_specs, check_vma=False)
```

time: 1500 us -> 141 us (0.09)
  waiting for transfers between devices: 924 us -> 0 us
  starting transfers between devices: 321 us -> 0 us
  Pallas kernels: 0 us -> 126 us
  local copies, waits for them, and re-layouts: 100 us -> 11 us
  matrix products: 69.3 us -> 0 us
  other arithmetic: 52.2 us -> 2.36 us
  loops' own time: 18.1 us -> 0 us
    ppermute x48 -> x0, waiting for transfers between devices: 918 us -> none  [the longest x16 844 us: shifted(): return lax.ppermute(shard, axis, pairs)]
    ppermute x48 -> x0, starting transfers between devices: 317 us -> none  [the longest x16 236 us: shifted(): return lax.ppermute(shard, axis, pairs)]
    pallas_call x0 -> x1, Pallas kernels: none -> 126 us  [shards(): pl.pallas_call(functools.partial(kernel, (S, Q, E, W, NB, BW, NG, GB)), o...]
    dot_general x27 -> x0, matrix products: 69.3 us -> none  [the longest x16 57.3 us: product(): jnp.einsum('ecgp,egop->ecgo', left_side, right_side, preferred_element_ty...]
    another operation x28 -> x1, local copies, waits for them, and re-layouts: 29.2 us -> 0.76 us  [shards(): owners.reshape(atoms, 1)]
    slice x33 -> x0, local copies, waits for them, and re-layouts: 23.8 us -> none  [the longest x4 7.68 us: through_inverse(): parted[:, 1]]
    another operation x18 -> x0, loops' own time: 18.1 us -> none  [the longest x1 16.9 us: shards(): lax.fori_loop(0, slabs, backward_turn, (jnp.zeros_like(left_lead), jnp.ze...]
    select_n x17 -> x0, other arithmetic: 15.3 us -> none  [the longest x8 10.7 us: forward_turn(): entering = jnp.where(leading, left_lead, arrived)]
  transfers between devices with their start and end apart: 49 -> 0, of which waited for: 49 -> 0; matrix products, arithmetic and copies ran while one was open for 0% -> 0% of each run, Pallas kernels for 0% -> 0%
where the time goes in v1:
time: 141 us; the launch traced here: 140 us
  Pallas kernels  126 us (89%)
  local copies, waits for them, and re-layouts  11 us (8%)
  other arithmetic  2.36 us (2%)
    pallas_call x1, Pallas kernels, shards(): pl.pallas_call(functools.partial(kernel, (S, Q, E, W, NB, BW, NG, GB)), o...  126 us
    unnamed x14, local copies, waits for them, and re-layouts  3.01 us
    transpose x1, local copies, waits for them, and re-layouts, shards(): mf = masked.transpose(1, 2, 4, 0, 3).reshape(NB, 3, BW, 2 * BW)  2.89 us
    reshape x1, local copies, waits for them, and re-layouts, shards(): mf = masked.transpose(1, 2, 4, 0, 3).reshape(NB, 3, BW, 2 * BW)  2.85 us

profile of v1, /device:TPU:0, one launch (start us, length us, event | category | flops | bytes accessed | tf_op | source)
XLA Modules:
  0.0 140.4 jit_solution(15044429031835750568)
XLA Ops:
  0.6 0.7 convert_element_type.11
  1.3 0.1 copy.15
  1.4 0.8 copy.14.own_col
  2.2 1.7 %fusion = (bf16[2,8,3,16,8,128]{5,4,3,2,1,0:T(8,128)(2,1)S(1)}, bf16[8,3,128,2,128]{2,4,1,0,3:T(8,128)(2,1)S(1)}) fusion(bf16[1,2,8,3,128,128]{5,4,3,2,1,0:T(8,128)(2,1)} %param.10, bf16[8,3]{1,0:T(8,128)(2,1)S(1)} %bitcast.30), kind=kLoop, calls=%fused_computation.2 | loop fusion | flops 786432 | bytes 4718640
  3.9 1.4 %copy.18 = bf16[2,8,3,16,8,128]{5,4,0,3,2,1:T(8,128)(2,1)} copy(bf16[2,8,3,16,8,128]{5,4,3,2,1,0:T(8,128)(2,1)S(1)} %get-tuple-element.6) | data formatting | bytes 3145728 | tf_op jit(solution)/shard_map/reshape | solution.py:293
  5.3 2.9 %copy.12 = bf16[8,3,128,2,128]{4,3,2,1,0:T(2,128)(2,1)} copy(bf16[8,3,128,2,128]{2,4,1,0,3:T(8,128)(2,1)S(1)} %get-tuple-element.7) | data formatting | bytes 3145728 | tf_op jit(solution)/shard_map/transpose | solution.py:294
  8.2 0.0 copy-start
  8.2 0.0 copy-start.2
  8.2 0.0 copy-start.3
  8.2 0.0 copy-start.4
  8.2 0.0 copy-start.5
  8.2 2.9 %reshape.30.mf = bf16[8,3,128,256]{3,2,1,0:T(8,128)(2,1)S(1)} reshape(bf16[8,3,128,2,128]{4,3,2,1,0:T(2,128)(2,1)} %copy.12) | data formatting | bytes 3145728 | tf_op jit(solution)/shard_map/reshape | solution.py:294
  11.1 0.0 copy-done
  11.1 0.0 copy-done.2
  11.1 0.0 copy-done.3
  11.1 0.0 copy-done.4
  11.1 0.0 copy-done.5
  11.1 0.0 copy-start.1
  11.1 1.2 copy-done.1
  12.4 126.3 %shard_map.104 = (bf16[4,128,1024]{2,1,0:T(8,128)(2,1)S(1)}, f32[8,128,128]{2,1,0:T(8,128)S(1)}) custom-call(bf16[4,2,2,512,512]{4,3,2,1,0:T(8,128)(2,1)} %bitcast.28, bf16[8,3,128,256]{3,2,1,0:T(8,128)(2,1)S(1)} %reshape.30.mf, bf16[8,3,128,256]{3,2,1,0:T(8,128)(2,1)} %bitcast.29, bf16[4,128,1024]{2,1,0:T(8,128)(2,1)S(1)} %bitcast.23, ...), custom_call_target="tpu_custom_call" | custom-call | tf_op jit(solution)/shard_map/pallas_call | solution.py:300
  138.7 1.0 copy.21
  139.6 0.8 copy.22
Async XLA Ops:
  8.2 2.9 %copy-start = (bf16[4,2,64,1024]{3,2,1,0:T(8,128)(2,1)S(1)}, bf16[4,2,64,1024]{3,2,1,0:T(8,128)(2,1)}, u32[]{:S(2)}) copy-start(bf16[4,2,64,1024]{3,2,1,0:T(8,128)(2,1)} %param.12) | copy-start | bytes 3145732
  8.2 2.9 %copy-start.2 = (f32[1,1024]{1,0:T(1,128)S(1)}, f32[1,1024]{1,0:T(1,128)}, u32[]{:S(2)}) copy-start(f32[1,1024]{1,0:T(1,128)} %pot.1) | copy-start | bytes 12292
  8.2 2.9 %copy-start.3 = (s32[1,128,1]{1,2,0:T(1,128)S(1)}, s32[1,128,1]{1,2,0:T(1,128)}, u32[]{:S(2)}) copy-start(s32[1,128,1]{1,2,0:T(1,128)} %param.17) | copy-start | bytes 1540
  8.2 2.9 %copy-start.4 = (f32[64]{0:T(128)S(1)}, f32[64]{0:T(128)}, u32[]{:S(2)}) copy-start(f32[64]{0:T(128)} %fermi.1) | copy-start | bytes 772
  8.2 2.9 %copy-start.5 = (s32[4]{0:T(128)S(1)}, s32[4]{0:T(128)}, u32[]{:S(2)}) copy-start(s32[4]{0:T(128)} %eidx.1) | copy-start | bytes 52
  11.1 1.2 copy-start.1

commit v2 on v1

--- a/solution.py
+++ b/solution.py
@@ -9,6 +9,7 @@
 
 ATOM_ORB = 8
 SCAP = 16
+LAG = 2
 F32 = jnp.float32
 BF16 = jnp.bfloat16
 
@@ -33,9 +34,9 @@
 
 def kernel(
     dims,
-    inv, mf, mb, left, right, pot, fermi, eidx, own_row, own_col,
+    inv, coup, left, right, pot, pattern, fermi, eidx, own_row,
     gout, rows_out,
-    ginv, xf, gf, xs, bb, stage, resp, sel, picked, sb, rb,
+    ginv, gturn, xf, gf, xs, mf, mb, bb, stage, resp, sel, picked, sb, rb,
     inv_sem, fs, fr, bs, br, cs, cr, ls, ts, tr,
 ):
     S, Q, E, W, NB, BW, NG, GB = dims
@@ -58,14 +59,24 @@
     def inv_copy(e):
         return here(inv.at[e], ginv.at[e], inv_sem.at[e])
 
-    def main(buf, e, g):
-        return buf.at[e, :, pl.ds(BW + g * GB, GB)]
+    pieces = [(0, 0, GB)]
+    for g in range(1, NG):
+        pieces += [(g, g * GB, BW), (g, g * GB + BW, GB - BW)]
+    NP = len(pieces)
+
+    def main(buf, e, p):
+        return buf.at[e, :, pl.ds(BW + pieces[p][1], pieces[p][2])]
+
+    def cut(src, e, p):
+        return src.at[e, :, pl.ds(pieces[p][1], pieces[p][2])]
 
     def halo(buf, e, side):
         return buf.at[e, :, pl.ds(0 if side == 0 else BW + W, BW)]
 
     def edge(src, e, side):
         return src.at[e, :, pl.ds(0 if side == 0 else W - BW, BW)]
+
+    early = s < 2
 
     def coupling_copies():
         out = [(None, to(mb.at[:, 1], bb.at[:, 1], cs.at[0], cr.at[0], -1, 0))]
@@ -77,17 +88,16 @@
         return out
 
     def wave_copies(src, dst, e, ssem, rsem, ds):
-        out = []
-        for g in range(NG):
-            out.append((None, g, to(src.at[e, :, pl.ds(g * GB, GB)], main(dst, e, g), ssem.at[e, g], rsem.at[e, g], ds, 0)))
-        out.append((~low, 0, to(edge(src, e, 0), halo(dst, e, 1), ssem.at[e, NG], rsem.at[e, NG + 1], ds, -1)))
-        out.append((~high, NG - 1, to(edge(src, e, 1), halo(dst, e, 0), ssem.at[e, NG + 1], rsem.at[e, NG], ds, 1)))
+        out = [(~high, NG - 1, to(edge(src, e, 1), halo(dst, e, 0), ssem.at[e, NP + 1], rsem.at[e, NP], ds, 1))]
+        for p in range(NP):
+            out.append((None, pieces[p][0], to(cut(src, e, p), main(dst, e, p), ssem.at[e, p], rsem.at[e, p], ds, 0)))
+        out.append((~low, 0, to(edge(src, e, 0), halo(dst, e, 1), ssem.at[e, NP], rsem.at[e, NP + 1], ds, -1)))
         return out
 
     def lead_copies(e):
         return [
-            (~low, to(edge(left, e, 0), halo(xf, e, 1), ls.at[e, 0], fr.at[e, NG + 1], 0, -1)),
-            (~high, to(edge(left, e, 1), halo(xf, e, 0), ls.at[e, 1], fr.at[e, NG], 0, 1)),
+            (~low, to(edge(left, e, 0), halo(xf, e, 1), ls.at[e, 0], fr.at[e, NP + 1], 0, -1)),
+            (~high, to(edge(left, e, 1), halo(xf, e, 0), ls.at[e, 1], fr.at[e, NP], 0, 1)),
         ]
 
     def guarded(cond, act):
@@ -96,13 +106,16 @@
         else:
             pl.when(cond)(act)
 
-    def await_wave(buf, e, rsem, halos):
-        for g in range(NG):
-            here(main(buf, e, g), main(buf, e, g), rsem.at[e, g]).wait()
-        if halos:
-            for side, edge_here in ((0, low), (1, high)):
+    def await_pieces(buf, e, rsem, g):
+        need = [2 * g] + ([2 * g + 1] if g + 1 < NG else [])
+        for p in need:
+            here(main(buf, e, p), main(buf, e, p), rsem.at[e, p]).wait()
+
+    def await_halos(buf, e, rsem, g):
+        for side, at, edge_here in ((0, 0, low), (1, NG - 1, high)):
+            if g == at:
                 h = halo(buf, e, side)
-                pl.when(~edge_here)(lambda h=h, side=side: here(h, h, rsem.at[e, NG + side]).wait())
+                pl.when(~edge_here)(lambda h=h, side=side: here(h, h, rsem.at[e, NP + side]).wait())
 
     def each_energy(body):
         def step(e, carry):
@@ -119,8 +132,8 @@
     def _():
         @each_energy
         def _(e):
-            for g in range(NG):
-                here(left.at[e, :, pl.ds(g * GB, GB)], main(xf, e, g), fr.at[e, g]).start()
+            for p in range(NP):
+                here(cut(left, e, p), main(xf, e, p), fr.at[e, p]).start()
             for cond, copy in lead_copies(e):
                 guarded(cond, copy.start)
 
@@ -128,13 +141,31 @@
     def _():
         @each_energy
         def _(e):
-            for g in range(NG):
-                here(right.at[e, :, pl.ds(g * GB, GB)], main(gf, e, g), br.at[e, g]).start()
+            for p in range(NP):
+                here(cut(right, e, p), main(gf, e, p), br.at[e, p]).start()
+
+    def mask_row(r, carry):
+        for d in range(3):
+            present = pattern[r * 3 + d].astype(F32)
+            for c in range(2):
+                block = (coup[c, r, d].astype(F32) * present).astype(BF16)
+                mb[r, d, :, pl.ds(c * BW, BW)] = block
+                mf[r, d, :, pl.ds(c * BW, BW)] = block.T
+        return carry
+
+    lax.fori_loop(0, NB, mask_row, 0)
 
     @pl.when(~first)
     def _():
         for cond, copy in coupling_copies():
             guarded(cond, copy.start)
+
+    def turn_inverses(e):
+        def turn(k, carry):
+            gturn[e, k // NG, k % NG] = ginv[e, k // NG, k % NG].T
+            return carry
+
+        lax.fori_loop(0, 2 * NG, turn, 0)
 
     zero = jnp.zeros((E, rows, BW), BF16)
     zero_block = jnp.zeros((BW, 2 * BW), BF16)
@@ -155,74 +186,84 @@
 
     atoms = own_row.shape[1]
     earlier = lax.broadcasted_iota(jnp.int32, (atoms, atoms), 0) < lax.broadcasted_iota(jnp.int32, (atoms, atoms), 1)
-    same = own_col[...] == own_row[...]
+    eye = lax.broadcasted_iota(jnp.int32, (atoms, atoms), 0) == lax.broadcasted_iota(jnp.int32, (atoms, atoms), 1)
+    own_col = jnp.sum(jnp.where(eye, own_row[...].astype(F32), 0.0), 1, keepdims=True)
+    same = own_col == own_row[...].astype(F32)
     rank = jnp.sum((same & earlier).astype(F32), 0, keepdims=True)
     place = lax.broadcasted_iota(jnp.int32, (S * SCAP, atoms), 0)
     rank_i = rank.astype(jnp.int32)
     wanted = own_row[...] * SCAP + rank_i
     sel[...] = jnp.where(place == wanted, 1.0, 0.0).astype(BF16)
 
-    def through(e, g, u):
-        dn = (((1,), (1,)), ((), ()))
-        return lax.dot_general(u, ginv[e, 0, g], dn, preferred_element_type=F32) + lax.dot_general(
-            turned(u, False), ginv[e, 1, g], dn, preferred_element_type=F32
-        )
-
-    def born(e, g):
+    def born(e, raw, g):
+        held = ginv if raw else gturn
+        dn = (((1,), (1 if raw else 0,)), ((), ()))
+
+        def through(u):
+            return lax.dot_general(u, held[e, 0, g], dn, preferred_element_type=F32) + lax.dot_general(
+                turned(u, False), held[e, 1, g], dn, preferred_element_type=F32
+            )
+
         u = stage[:, pl.ds(g * GB, GB)]
-        gain = through(e, g, u).astype(BF16).astype(F32)
+        gain = through(u).astype(BF16).astype(F32)
         mix = (u.astype(F32) + pot[:, pl.ds(g * GB, GB)] * gain).astype(BF16)
-        return through(e, g, mix)
-
-    def couple(buf, e, weights, conj):
-        for b in range(NB):
+        return through(mix)
+
+    def couple(buf, e, weights, g, conj):
+        per = GB // BW
+        for b in range(g * per, (g + 1) * per):
             window = buf[e, :, pl.ds(b * BW, 3 * BW)]
             stage[:, pl.ds(b * BW, BW)] = coupled(window, weights[b].reshape(3 * BW, 2 * BW), conj)
 
-    def forward(e):
-        inv_copy(e).wait()
-        await_wave(xf, e, fr, True)
-        couple(xf, e, mf, False)
+    def send(copies, g, cond):
+        @pl.when(cond)
+        def _():
+            for c, after, copy in copies:
+                if after == g:
+                    guarded(c, copy.start)
+
+    @pl.when(~early)
+    def _():
+        @each_energy
+        def _(e):
+            inv_copy(e).wait()
+            turn_inverses(e)
+
+    def forward(e, raw):
+        if raw:
+            inv_copy(e).wait()
         copies = wave_copies(xs, xf, e, fs, fr, 1)
         for g in range(NG):
-            xs[e, :, pl.ds(g * GB, GB)] = born(e, g).astype(BF16)
-
-            @pl.when(~last)
-            def _():
-                for cond, after, copy in copies:
-                    if after == g:
-                        guarded(cond, copy.start)
-
-    each_energy(forward)
-
-    @pl.when(~last)
-    def _():
-        for i, region in enumerate((bb.at[:, 1], bb.at[pl.ds(0, NB - 1), 2], bb.at[pl.ds(1, NB - 1), 0])):
-            here(region, region, cr.at[i]).wait()
-        pl.when(~high)(lambda: here(bb.at[NB - 1, 2], bb.at[NB - 1, 2], cr.at[3]).wait())
-        pl.when(~low)(lambda: here(bb.at[0, 0], bb.at[0, 0], cr.at[4]).wait())
+            await_pieces(xf, e, fr, g)
+            await_halos(xf, e, fr, g)
+            couple(xf, e, mf, g, False)
+            xs[e, :, pl.ds(g * GB, GB)] = born(e, raw, g).astype(BF16)
+            send(copies, g, ~last)
 
     def backward(e):
-        @pl.when(last)
+        @pl.when(~last & (e == 0))
         def _():
-            await_wave(gf, e, br, False)
-            stage[...] = gf[e, :, pl.ds(BW, W)]
-
-        @pl.when(~last)
-        def _():
-            await_wave(gf, e, br, True)
-            couple(gf, e, bb, True)
+            for i, region in enumerate((bb.at[:, 1], bb.at[pl.ds(0, NB - 1), 2], bb.at[pl.ds(1, NB - 1), 0])):
+                here(region, region, cr.at[i]).wait()
+            pl.when(~high)(lambda: here(bb.at[NB - 1, 2], bb.at[NB - 1, 2], cr.at[3]).wait())
+            pl.when(~low)(lambda: here(bb.at[0, 0], bb.at[0, 0], cr.at[4]).wait())
 
         copies = wave_copies(gout, gf, e, bs, br, -1)
         for g in range(NG):
             cols = pl.ds(g * GB, GB)
-            gout[e, :, cols] = (xs[e, :, cols].astype(F32) + born(e, g)).astype(BF16)
-
-            @pl.when(~first)
+            await_pieces(gf, e, br, g)
+
+            @pl.when(last)
             def _():
-                for cond, after, copy in copies:
-                    if after == g:
-                        guarded(cond, copy.start)
+                stage[:, cols] = gf[e, :, pl.ds(BW + g * GB, GB)]
+
+            @pl.when(~last)
+            def _():
+                await_halos(gf, e, br, g)
+                couple(gf, e, bb, g, True)
+
+            gout[e, :, cols] = (xs[e, :, cols].astype(F32) + born(e, False, g)).astype(BF16)
+            send(copies, g, ~first)
 
         weight = fermi[eidx[e]]
         for b in range(NB):
@@ -230,7 +271,17 @@
             gram = lax.dot_general(a, a, (((0,), (0,)), ((), ())), preferred_element_type=F32)
             resp[pl.ds(b * BW, BW), :] += weight * gram
 
-    each_energy(backward)
+    lag = jnp.where(last, 0, jnp.where(s == S - 2, min(LAG, E), E))
+
+    def slot(t, carry):
+        e = lax.rem(t, E)
+        pl.when((t < E) & early)(lambda: forward(e, True))
+        pl.when((t < E) & ~early)(lambda: forward(e, False))
+        pl.when((t == E) & early)(lambda: each_energy(turn_inverses))
+        pl.when((t >= lag) & (t < lag + E))(lambda: backward(lax.rem(t + 2 * E - lag, E)))
+        return carry
+
+    lax.fori_loop(0, 2 * E, slot, 0)
 
     for x in range(ATOM_ORB):
         part = (resp[pl.ds(x, atoms, stride=ATOM_ORB), :] * (1.0 / rows)).astype(BF16)
@@ -289,9 +340,6 @@
     NG, GB = inverses.shape[3], inverses.shape[4]
     rows = 2 * modes
     atoms = owner_map.shape[1]
-    masked = coupling[0] * pattern[0][None, :, :, None, None].astype(BF16)
-    mb = masked.transpose(1, 2, 3, 0, 4).reshape(NB, 3, BW, 2 * BW)
-    mf = masked.transpose(1, 2, 4, 0, 3).reshape(NB, 3, BW, 2 * BW)
     owners = owner_map.reshape(atoms)
     vm = pl.BlockSpec(memory_space=pltpu.VMEM)
     sm = pl.BlockSpec(memory_space=pltpu.SMEM)
@@ -303,13 +351,16 @@
             jax.ShapeDtypeStruct((E, rows, W), BF16),
             jax.ShapeDtypeStruct((S, SCAP * ATOM_ORB, BW), F32),
         ),
-        in_specs=[hbm, vm, vm, hbm, hbm, vm, sm, sm, vm, vm],
+        in_specs=[hbm, vm, hbm, hbm, vm, sm, sm, sm, vm],
         out_specs=(vm, vm),
         scratch_shapes=[
+            pltpu.VMEM((E, 2, NG, GB, GB), BF16),
             pltpu.VMEM((E, 2, NG, GB, GB), BF16),
             pltpu.VMEM((E, rows, W + 2 * BW), BF16),
             pltpu.VMEM((E, rows, W + 2 * BW), BF16),
             pltpu.VMEM((E, rows, W), BF16),
+            pltpu.VMEM((NB, 3, BW, 2 * BW), BF16),
+            pltpu.VMEM((NB, 3, BW, 2 * BW), BF16),
             pltpu.VMEM((NB, 3, BW, 2 * BW), BF16),
             pltpu.VMEM((rows, W), BF16),
             pltpu.VMEM((W, BW), F32),
@@ -318,10 +369,10 @@
             pltpu.VMEM((S, SCAP * ATOM_ORB, BW), BF16),
             pltpu.VMEM((S, SCAP * ATOM_ORB, BW), BF16),
             dma((E,)),
-            dma((E, NG + 2)),
-            dma((E, NG + 2)),
-            dma((E, NG + 2)),
-            dma((E, NG + 2)),
+            dma((E, 2 * NG + 1)),
+            dma((E, 2 * NG + 1)),
+            dma((E, 2 * NG + 1)),
+            dma((E, 2 * NG + 1)),
             dma((5,)),
             dma((5,)),
             dma((E, 2)),
@@ -331,15 +382,14 @@
         compiler_params=pltpu.CompilerParams(has_side_effects=True, vmem_limit_bytes=48 * 2**20),
     )(
         inverses[0],
-        mf,
-        mb,
+        coupling[0],
         left_lead.reshape(E, rows, W),
         right_lead.reshape(E, rows, W),
         potential,
+        pattern.reshape(NB * 3),
         fermi_weight,
         energy_index,
         owners.reshape(1, atoms),
-        owners.reshape(atoms, 1),
     )
     return (
         green.reshape(1, E, 2, modes, W),

time: 141 us -> 109 us (0.77)
  Pallas kernels: 126 us -> 97.7 us
  other arithmetic: 2.36 us -> 0 us
  local copies, waits for them, and re-layouts: 11 us -> 9.11 us
    pallas_call x1, Pallas kernels: 126 us -> 97.7 us  [shards(): pl.pallas_call(functools.partial(kernel, (S, Q, E, W, NB, BW, NG, GB)), o...]
    unnamed x14 -> x17, local copies, waits for them, and re-layouts: 3.01 us -> 9.03 us
    reshape x2 -> x1, local copies, waits for them, and re-layouts: 4.29 us -> 0.08 us  [shards(): pattern.reshape(NB * 3)]
    transpose x1 -> x0, local copies, waits for them, and re-layouts: 2.89 us -> none  [shards(): mf = masked.transpose(1, 2, 4, 0, 3).reshape(NB, 3, BW, 2 * BW)]
    unnamed x1 -> x0, other arithmetic: 1.68 us -> none
where the time goes in v2:
time: 109 us; the launch traced here: 107 us
  Pallas kernels  97.7 us (90%)
  local copies, waits for them, and re-layouts  9.11 us (8%)
    pallas_call x1, Pallas kernels, shards(): pl.pallas_call(functools.partial(kernel, (S, Q, E, W, NB, BW, NG, GB)), o...  97.7 us
    unnamed x17, local copies, waits for them, and re-layouts  9.03 us

profile of v2, /device:TPU:0, one launch (start us, length us, event | category | flops | bytes accessed | tf_op | source)
XLA Modules:
  0.0 107.4 jit_solution(5517105471381649892)
XLA Ops:
  0.6 0.8 copy.12
  1.4 0.1 reshape.21.pattern
  1.5 0.0 copy-start
  1.5 1.4 %copy-done = bf16[1,2,8,3,128,128]{5,4,3,2,1,0:T(8,128)(2,1)S(1)} copy-done((bf16[1,2,8,3,128,128]{5,4,3,2,1,0:T(8,128)(2,1)S(1)}, bf16[1,2,8,3,128,128]{5,4,3,2,1,0:T(8,128)(2,1)}, u32[]{:S(2)}) %copy-start) | copy-done | bytes 1572888
  2.9 0.0 copy-start.1
  2.9 1.2 %copy-done.1 = bf16[4,2,64,1024]{3,2,1,0:T(8,128)(2,1)S(1)} copy-done((bf16[4,2,64,1024]{3,2,1,0:T(8,128)(2,1)S(1)}, bf16[4,2,64,1024]{3,2,1,0:T(8,128)(2,1)}, u32[]{:S(2)}) %copy-start.1) | copy-done | bytes 1048600
  4.1 0.0 copy-start.2
  4.1 1.2 %copy-done.2 = bf16[4,2,64,1024]{3,2,1,0:T(8,128)(2,1)S(1)} copy-done((bf16[4,2,64,1024]{3,2,1,0:T(8,128)(2,1)S(1)}, bf16[4,2,64,1024]{3,2,1,0:T(8,128)(2,1)}, u32[]{:S(2)}) %copy-start.2) | copy-done | bytes 1048600
  5.3 0.0 copy-start.3
  5.3 0.7 copy-done.3
  6.0 0.0 copy-start.4
  6.0 0.7 copy-done.4
  6.7 0.0 copy-start.5
  6.7 0.7 copy-done.5
  7.3 0.0 copy-start.6
  7.3 0.7 copy-done.6
  8.0 97.7 %shard_map.104 = (bf16[4,128,1024]{2,1,0:T(8,128)(2,1)S(1)}, f32[8,128,128]{2,1,0:T(8,128)S(1)}) custom-call(bf16[4,2,2,512,512]{4,3,2,1,0:T(8,128)(2,1)} %bitcast.13, bf16[2,8,3,128,128]{4,3,2,1,0:T(8,128)(2,1)S(1)} %bitcast.7, bf16[4,128,1024]{2,1,0:T(8,128)(2,1)S(1)} %bitcast.8, bf16[4,128,1024]{2,1,0:T(8,128)(2,1)S(1)} %bitcast.9, ...), custom_call_target="tpu_custom_call" | custom-call | tf_op jit(solution)/shard_map/pallas_call | solution.py:348
  105.7 1.0 copy.15
  106.7 0.8 copy.16
Async XLA Ops:
  1.5 1.4 %copy-start = (bf16[1,2,8,3,128,128]{5,4,3,2,1,0:T(8,128)(2,1)S(1)}, bf16[1,2,8,3,128,128]{5,4,3,2,1,0:T(8,128)(2,1)}, u32[]{:S(2)}) copy-start(bf16[1,2,8,3,128,128]{5,4,3,2,1,0:T(8,128)(2,1)} %param.10) | copy-start | bytes 4718596
  2.9 1.2 %copy-start.1 = (bf16[4,2,64,1024]{3,2,1,0:T(8,128)(2,1)S(1)}, bf16[4,2,64,1024]{3,2,1,0:T(8,128)(2,1)}, u32[]{:S(2)}) copy-start(bf16[4,2,64,1024]{3,2,1,0:T(8,128)(2,1)} %param.12) | copy-start | bytes 3145732
  4.1 1.2 %copy-start.2 = (bf16[4,2,64,1024]{3,2,1,0:T(8,128)(2,1)S(1)}, bf16[4,2,64,1024]{3,2,1,0:T(8,128)(2,1)}, u32[]{:S(2)}) copy-start(bf16[4,2,64,1024]{3,2,1,0:T(8,128)(2,1)} %param.13) | copy-start | bytes 3145732
  5.3 0.7 copy-start.3
  6.0 0.7 copy-start.4
  6.7 0.7 copy-start.5
  7.3 0.7 copy-start.6

commit v3 on v2

--- a/solution.py
+++ b/solution.py
@@ -379,7 +379,7 @@
             dma((S,)),
             dma((S,)),
         ],
-        compiler_params=pltpu.CompilerParams(has_side_effects=True, vmem_limit_bytes=48 * 2**20),
+        compiler_params=pltpu.CompilerParams(has_side_effects=True, vmem_limit_bytes=60 * 2**20),
     )(
         inverses[0],
         coupling[0],

time: 109 us -> 107 us (0.982)
  local copies, waits for them, and re-layouts: 9.11 us -> 5.48 us
  Pallas kernels: 97.7 us -> 99.5 us
    unnamed x17 -> x3, local copies, waits for them, and re-layouts: 9.03 us -> 4.89 us
    pallas_call x1, Pallas kernels: 97.7 us -> 99.5 us  [shards(): pl.pallas_call(functools.partial(kernel, (S, Q, E, W, NB, BW, NG, GB)), o...]
where the time goes in v3:
time: 107 us; the launch traced here: 106 us
  Pallas kernels  99.5 us (93%)
  local copies, waits for them, and re-layouts  5.48 us (5%)
    pallas_call x1, Pallas kernels, shards(): pl.pallas_call(functools.partial(kernel, (S, Q, E, W, NB, BW, NG, GB)), o...  99.5 us
    unnamed x3, local copies, waits for them, and re-layouts  4.89 us

profile of v3, /device:TPU:0, one launch (start us, length us, event | category | flops | bytes accessed | tf_op | source)
XLA Modules:
  0.0 105.6 jit_solution(6988410849848716024)
XLA Ops:
  0.6 0.8 copy.12
  1.4 0.6 reshape.21.pattern
  2.0 99.5 %shard_map.104 = (bf16[4,128,1024]{2,1,0:T(8,128)(2,1)}, f32[8,128,128]{2,1,0:T(8,128)}) custom-call(bf16[4,2,2,512,512]{4,3,2,1,0:T(8,128)(2,1)} %bitcast.7, bf16[2,8,3,128,128]{4,3,2,1,0:T(8,128)(2,1)} %bitcast.8, bf16[4,128,1024]{2,1,0:T(8,128)(2,1)} %bitcast.9, bf16[4,128,1024]{2,1,0:T(8,128)(2,1)} %bitcast.10, f32[1,1024]{1,0:T(1,128)} %pot.1, ...), custom_call_target="tpu_custom_call" | custom-call | tf_op jit(solution)/shard_map/pallas_call | solution.py:348
  101.5 2.3 %copy.15 = bf16[1,4,2,64,1024]{4,3,2,1,0:T(8,128)(2,1)} copy(bf16[1,4,2,64,1024]{4,3,2,1,0:T(8,128)(2,1)} %bitcast.11) | data formatting | bytes 2097152
  103.7 1.9 %copy.16 = f32[1,8,16,8,128]{4,3,2,1,0:T(8,128)} copy(f32[1,8,16,8,128]{4,3,2,1,0:T(8,128)} %bitcast.12) | data formatting | bytes 1048576
